TPU v7x, 32 devices: a whole 2x2x4 slice. The times are simulated.
32 devices in a mesh: replica: 4 (over y, x), shard: 8 (over z, core).
Axes of the slice: x: 2, y: 2, z: 4, core: 2. Of those that a mesh axis runs over, the one named last changes fastest.
Arguments:
- hidden: bfloat16 [2, 32, 256, 768], P(None, ('replica', 'shard')), may hold values from -6 to 6
- encoded: bfloat16 [2, 32, 256, 768], P(None, ('replica', 'shard')), may hold values from -6 to 6
- out_grad: bfloat16 [2, 32, 256, 768], P(None, ('replica', 'shard')), may hold values from -6 to 6
- seg_start: int32 [2, 32, 13], P(None, ('replica', 'shard')), may hold values from 0 to 240, as said below
- seg_parent: int32 [2, 32, 13], P(None, ('replica', 'shard')), may hold values from 0 to 4, as said below
- bucket_of_distance: int32 [256], replicated, may hold values from 0 to 31, as said below
- norm_self: bfloat16 [768], P('shard'), may hold values from 0.5 to 1.5
- self_query: bfloat16 [768, 768], P('shard'), may hold values from -0.109375 to 0.109375
- self_key: bfloat16 [768, 768], P('shard'), may hold values from -0.109375 to 0.109375
- self_value: bfloat16 [768, 768], P('shard'), may hold values from -0.21875 to 0.21875
- self_out: bfloat16 [768, 768], P('shard'), may hold values from -0.875 to 0.875
- rel_bias: bfloat16 [32, 12], P('shard'), may hold values from -4 to 4
- norm_cross: bfloat16 [768], P('shard'), may hold values from 0.5 to 1.5
- cross_query: bfloat16 [768, 768], P('shard'), may hold values from -0.109375 to 0.109375
- cross_key: bfloat16 [768, 768], P('shard'), may hold values from -0.109375 to 0.109375
- cross_value: bfloat16 [768, 768], P('shard'), may hold values from -0.21875 to 0.21875
- cross_out: bfloat16 [768, 768], P('shard'), may hold values from -0.875 to 0.875
- norm_ff: bfloat16 [768], P('shard'), may hold values from 0.5 to 1.5
- ff_gate: bfloat16 [768, 2048], P('shard'), may hold values from -0.21875 to 0.21875
- ff_up: bfloat16 [768, 2048], P('shard'), may hold values from -0.21875 to 0.21875
- ff_down: bfloat16 [2048, 768], P('shard'), may hold values from -0.125 to 0.125
Outputs:
- layer_out: bfloat16 [2, 32, 256, 768], P(None, ('replica', 'shard'))
- grad_hidden: bfloat16 [2, 32, 256, 768], P(None, ('replica', 'shard'))
- grad_encoded: bfloat16 [2, 32, 256, 768], P(None, ('replica', 'shard'))
- grad_norm_self: float32 [768], P('shard')
- grad_self_query: float32 [768, 768], P('shard')
- grad_self_key: float32 [768, 768], P('shard')
- grad_self_value: float32 [768, 768], P('shard')
- grad_self_out: float32 [768, 768], P('shard')
- grad_rel_bias: float32 [32, 12], P('shard')
- grad_norm_cross: float32 [768], P('shard')
- grad_cross_query: float32 [768, 768], P('shard')
- grad_cross_key: float32 [768, 768], P('shard')
- grad_cross_value: float32 [768, 768], P('shard')
- grad_cross_out: float32 [768, 768], P('shard')
- grad_norm_ff: float32 [768], P('shard')
- grad_ff_gate: float32 [768, 2048], P('shard')
- grad_ff_up: float32 [768, 2048], P('shard')
- grad_ff_down: float32 [2048, 768], P('shard')
Inputs may be any that keep to these rules, and one draw needn't show every extreme that they name: `seg_start`: segment 0 is the trunk and starts at 0; the twelve other segments lie end to end after it in some order, each once. `seg_parent`: segments 0 to 4 have parent 0; each of segments 1 to 4 is the parent of exactly two of segments 5 to 12. `bucket_of_distance`: entry 0 is 0; from one distance to the next it rises by 1 or 2 until it reaches 31, and then stays.
All inputs are finite; a program needn't handle non-finite values.
Results may differ from a plain program's by a relative error of at most 0.03.
The roundings to bfloat16 on the way count: a program that leaves them out, or rounds other values in their place, can miss the bound.
Values may be sent and summed in bfloat16 or wider, within the bound.
A program may use at most 192 MiB of HBM per device.

v0:
```python
import functools
import math

import jax
import jax.numpy as jnp
from jax import lax
from jax.experimental import pallas as pl
from jax.experimental.pallas import tpu as pltpu
from jax.sharding import PartitionSpec as P

SQ, FFN, H, DH, TREE, NSEG, NB = 768, 2048, 12, 64, 256, 13, 32
TRUNK, BRANCH, LEAF = 64, 16, 16
BF, F32 = jnp.bfloat16, jnp.float32
EPSILON, NEGATIVE = 1e-6, -1e9
DEPTHS = 128
SEG_LEN = (TRUNK,) + (BRANCH,) * 4 + (LEAF,) * 8
SEG_DEPTH = (0,) + (TRUNK,) * 4 + (TRUNK + BRANCH,) * 8

def nn(a, b): return lax.dot_general(a, b, (((1,), (0,)), ((), ())), preferred_element_type=F32)
def nt(a, b): return lax.dot_general(a, b, (((1,), (1,)), ((), ())), preferred_element_type=F32)
def tn(a, b): return lax.dot_general(a, b, (((0,), (0,)), ((), ())), preferred_element_type=F32)

class Layer:
    def __init__(self, refs, trees):
        self.__dict__.update(refs)
        self.trees = trees
        self.tokens = trees * TREE

    def layout(self):
        for t in range(self.trees):
            def place(shape, axis):
                pos = lax.broadcasted_iota(jnp.int32, shape, axis)
                dep, sid, pid, gid = pos, jnp.zeros_like(pos), jnp.zeros_like(pos), jnp.zeros_like(pos)
                for s in range(NSEG):
                    at = self.seg_start[t, s]
                    inside = (pos >= at) & (pos < at + SEG_LEN[s])
                    dep = dep + jnp.where(inside, SEG_DEPTH[s] - at, 0)
                    sid = jnp.where(inside, s, sid)
                    pid = jnp.where(inside, self.seg_parent[t, s], pid)
                    gid = jnp.where(inside, self.seg_parent[t, self.seg_parent[t, s]], gid)
                return dep, sid, pid, gid
            dep_j, sid_j, _, _ = place((TREE, 1), 0)
            dep_i, sid_i, pid_i, gid_i = place((1, TREE), 1)
            ok = ((sid_j == sid_i) | (sid_j == pid_i) | (sid_j == gid_i)) & (dep_j <= dep_i)
            self.mask[t] = jnp.where(ok, 0.0, NEGATIVE).astype(F32)
            lanes = lax.broadcasted_iota(jnp.int32, (TREE, DEPTHS), 1)
            self.hot[t] = jnp.where(lanes == dep_j, 1.0, 0.0).astype(BF)
            rows = lax.broadcasted_iota(jnp.int32, (DEPTHS, TREE), 0)
            self.hot_t[t] = jnp.where(rows == DEPTHS - 1 - dep_i, 1.0, 0.0).astype(BF)

    def bucket_hot(self):
        row = lax.broadcasted_iota(jnp.int32, (128, DEPTHS), 0)
        inner = row % 16
        bucket = jnp.where((inner >= 4) & (inner < 8), 4 * (row // 16) + inner - 4, -1)
        return jnp.where(self.bucket[...][:1] == bucket, 1.0, 0.0).astype(BF)

    def spread(self, s):
        i = lax.broadcasted_iota(jnp.int32, (128, SQ), 0)
        j = lax.broadcasted_iota(jnp.int32, (128, SQ), 1)
        return jnp.where((j == i + 96 * s) & (i < 96), 1.0, 0.0).astype(BF)

    def small_params(self):
        total = jnp.zeros((16, SQ), F32)
        for s in range(8):
            total = total + nn(self.small[s], self.spread(s))
        self.gains[...] = total
        table = tn(self.small[...].reshape(128, 128), self.bucket_hot())
        for h in range(H):
            row = jnp.broadcast_to(table[h:h + 1], (DEPTHS, DEPTHS))
            self.toep[h] = pltpu.roll(row, 0, 1, stride=1, stride_axis=0).astype(BF)
        self.gain_grads[...] = jnp.zeros_like(self.gain_grads)
        self.bias_grads[...] = jnp.zeros_like(self.bias_grads)

    def small_grads(self):
        hot = self.bucket_hot()
        sums = self.bias_grads[...]
        high = sums.astype(BF)
        low = (sums - high.astype(F32)).astype(BF)
        out = nt(hot, high) + nt(hot, low)
        gains = self.gain_grads[...].astype(BF)
        for s in range(8):
            self.small_out[s] = (out[16 * s:16 * s + 16] + nt(gains, self.spread(s))).astype(BF)

    def norm(self, src, dst, gain):
        g = self.gains[gain:gain + 1, :]
        @pl.loop(0, self.tokens // 64, unroll=4)
        def _(b):
            rows = pl.ds(b * 64, 64)
            v = src[rows, :].astype(F32)
            r = lax.rsqrt(jnp.mean(v * v, axis=-1, keepdims=True) + EPSILON)
            dst[rows, :] = (v * r * g).astype(BF)

    def norm_back(self, src, gain, store):
        g = self.gains[gain:gain + 1, :]
        @pl.loop(0, self.tokens // 64, unroll=4)
        def _(b):
            rows = pl.ds(b * 64, 64)
            v = src[rows, :].astype(F32)
            r = lax.rsqrt(jnp.mean(v * v, axis=-1, keepdims=True) + EPSILON)
            n = v * r
            dh = self.gn[rows, :]
            dg = dh * g
            self.gain_grads[gain:gain + 1, :] += jnp.sum(dh * n, axis=0, keepdims=True)
            store(rows, r * (dg - n * jnp.mean(dg * n, axis=-1, keepdims=True)))

    def wsq(self, w): return self.sq[w].reshape(SQ, SQ)
    def project(self, src, w, dst):
        @pl.loop(0, 3, unroll=3)
        def _(n):
            cols = pl.ds(pl.multiple_of(n * 256, 256), 256)
            wt = self.sq[w, :, :, :, cols].reshape(SQ, 256)
            for t in range(self.trees):
                rows = pl.ds(t * TREE, TREE)
                dst[rows, cols] = nn(src[rows, :], wt).astype(BF)
    def project_add(self, src, w, base, dst):
        @pl.loop(0, 3, unroll=3)
        def _(n):
            cols = pl.ds(pl.multiple_of(n * 256, 256), 256)
            wt = self.sq[w, :, :, :, cols].reshape(SQ, 256)
            for t in range(self.trees):
                rows = pl.ds(t * TREE, TREE)
                dst[rows, cols] = base[rows, cols].astype(F32) + nn(src[rows, :], wt)
    def back(self, pairs, dst, dtype):
        @pl.loop(0, 2, unroll=2)
        def _(n):
            cols = pl.ds(pl.multiple_of(n * 384, 384), 384)
            for t in range(self.trees):
                rows = pl.ds(t * TREE, TREE)
                total = None
                for src, w in pairs:
                    part = nt(src[rows, :], self.sq[w, pl.ds(n * 2, 2)].reshape(384, SQ))
                    total = part if total is None else total + part
                dst[rows, cols] = total.astype(dtype)
    def weight_grad(self, left, right, w):
        @pl.loop(0, 2, unroll=2)
        def _(n):
            cols = pl.ds(pl.multiple_of(n * 384, 384), 384)
            lt = left[:, cols]
            for m in range(3):
                part = tn(lt, right[:, m * 256:(m + 1) * 256])
                self.sq[w, pl.ds(n * 2, 2), :, :, m * 256:(m + 1) * 256] = part.astype(BF).reshape(2, 2, 96, 256)

    def lanes(self):
        low = lax.broadcasted_iota(jnp.int32, (TREE, 128), 1) < DH
        return low, jnp.logical_not(low)
    def attend(self, q, k, v, ctx, probs, masked, first, last):
        halves = self.lanes()
        @pl.loop(first * self.trees // 2, last * self.trees // 2, unroll=3)
        def _(i):
            t, p = i // (H // 2), i % (H // 2)
            rows = pl.ds(pl.multiple_of(t * TREE, TREE), TREE)
            cols = pl.ds(pl.multiple_of(p * 128, 128), 128)
            qp, kp, vt = q[rows, cols], k[rows, cols], v[rows, cols].T
            if masked:
                hot = self.hot[t]
                kp = jnp.concatenate([kp, hot], axis=1)
            outs = []
            for e in range(2):
                qe = jnp.where(halves[e], qp, jnp.zeros_like(qp))
                if masked:
                    qe = jnp.concatenate([qe, nt(hot, self.toep[2 * p + e]).astype(BF)], axis=1)
                s = nt(kp, qe)
                if masked:
                    s = s + self.mask[t]
                x = jnp.exp(s - jnp.max(s, axis=0, keepdims=True))
                pr = (x * (1.0 / jnp.sum(x, axis=0, keepdims=True))).astype(BF)
                probs[2 * i + e] = pr
                outs.append(nn(vt[e * DH:(e + 1) * DH], pr))
            ctx[rows, cols] = jnp.concatenate(outs, axis=0).astype(BF).T
    def attend_back(self, q, k, v, dctx, probs, masked, first, last):
        halves = self.lanes()
        @pl.loop(first * self.trees // 2, last * self.trees // 2, unroll=3)
        def _(i):
            t, p = i // (H // 2), i % (H // 2)
            rows = pl.ds(pl.multiple_of(t * TREE, TREE), TREE)
            cols = pl.ds(pl.multiple_of(p * 128, 128), 128)
            qp, kt, vp, dp = q[rows, cols], k[rows, cols].T, v[rows, cols], dctx[rows, cols]
            dq, dk, dv = [], [], []
            for e in range(2):
                pr = probs[2 * i + e]
                prf = pr.astype(F32)
                g = nt(vp, jnp.where(halves[e], dp, jnp.zeros_like(dp)))
                ds = (prf * (g - jnp.sum(g * prf, axis=0, keepdims=True))).astype(BF)
                dv.append(nn(pr, dp))
                dq.append(nn(kt[e * DH:(e + 1) * DH], ds))
                dk.append(nn(ds, qp))
                if masked:
                    m = nn(nn(self.hot_t[t], ds).astype(BF), self.hot[t])
                    m = pltpu.roll(m, 1, 1, stride=1, stride_axis=0)
                    self.bias_grads[pl.ds(2 * p + e, 1), :] += jnp.sum(m, axis=0, keepdims=True)
            q[rows, cols] = jnp.concatenate(dq, axis=0).astype(BF).T
            k[rows, cols] = jnp.where(halves[0], dk[0], dk[1]).astype(BF)
            v[rows, cols] = jnp.where(halves[0], dv[0], dv[1]).astype(BF)

    def feed_forward(self, m):
        base = pl.multiple_of(m * 512, 512)
        for hf in range(2):
            cols = pl.ds(pl.multiple_of(base + hf * 256, 256), 256)
            wg = self.gu[0, :, :, :, :, cols].reshape(SQ, 256)
            wu = self.gu[1, :, :, :, :, cols].reshape(SQ, 256)
            wd = self.dn[m, hf].reshape(256, SQ)
            here = slice(hf * 256, hf * 256 + 256)
            @pl.loop(0, self.trees, unroll=2)
            def _(t):
                rows = pl.ds(pl.multiple_of(t * TREE, TREE), TREE)
                x = self.nf[rows, :]
                g, u, gi = nn(x, wg), nn(x, wu), nt(self.dy[rows, :], wd)
                c = math.sqrt(2.0 / math.pi)
                th = jnp.tanh(c * (g + 0.044715 * (g * g * g)))
                half = 0.5 * (1.0 + th)
                gelu = g * half
                slope = half + 0.5 * g * (1.0 - th * th) * c * (1.0 + 3 * 0.044715 * (g * g))
                self.inner[rows, here] = (gelu * u).astype(BF)
                self.ggate[rows, here] = (gi * u * slope).astype(BF)
                self.gup[rows, here] = (gi * gelu).astype(BF)
        @pl.loop(0, 3, unroll=3)
        def _(n):
            cols = pl.ds(pl.multiple_of(n * 256, 256), 256)
            wd = self.dn[m, :, :, :, cols].reshape(512, 256)
            for t in range(self.trees):
                rows = pl.ds(t * TREE, TREE)
                self.oacc[rows, cols] += nn(self.inner[rows, :], wd)
        @pl.loop(0, 2, unroll=2)
        def _(n):
            cols = pl.ds(pl.multiple_of(n * 384, 384), 384)
            hid = pl.ds(base, 512)
            wg = self.gu[0, pl.ds(n * 2, 2), :, :, :, hid].reshape(384, 512)
            wu = self.gu[1, pl.ds(n * 2, 2), :, :, :, hid].reshape(384, 512)
            for t in range(self.trees):
                rows = pl.ds(t * TREE, TREE)
                self.gn[rows, cols] += nt(self.ggate[rows, :], wg) + nt(self.gup[rows, :], wu)
        @pl.loop(0, 2, unroll=2)
        def _(n):
            hid = pl.ds(base, 512)
            cols = pl.ds(pl.multiple_of(n * 384, 384), 384)
            lt = self.nf[:, cols]
            self.gu[0, pl.ds(n * 2, 2), :, :, :, hid] = tn(lt, self.ggate[...]).astype(BF).reshape(2, 2, 2, 48, 512)
            self.gu[1, pl.ds(n * 2, 2), :, :, :, hid] = tn(lt, self.gup[...]).astype(BF).reshape(2, 2, 2, 48, 512)
        @pl.loop(0, 3, unroll=3)
        def _(n):
            cols = pl.ds(pl.multiple_of(n * 256, 256), 256)
            self.dn[m, :, :, :, cols] = tn(self.inner[...], self.dy[:, cols]).astype(BF).reshape(2, 4, 64, 256)

    def start_ff(self):
        self.norm(self.after_cross, self.nf, 2)
        self.oacc[...] = self.after_cross[...]
        self.gn[...] = jnp.zeros_like(self.gn)
    def end_ff(self):
        self.stage[...] = self.oacc[...].astype(BF)
    def back_ff_norm(self):
        def store(rows, dv):
            total = self.dy[rows, :].astype(F32) + dv
            self.oacc[rows, :] = total
            self.gb[rows, :] = total.astype(BF)
        self.norm_back(self.after_cross, 2, store)
    def back_cross_a(self):
        self.weight_grad_after(self.cctx, self.gb, 7, self.cctx)
    def weight_grad_after(self, ctx, grad, w, dst):
        self.back([(grad, w)], self.stage, BF)
        self.weight_grad(ctx, grad, w)
        dst[...] = self.stage[...]
    def back_cross_norm(self):
        def store(rows, dv):
            total = self.oacc[rows, :] + dv
            self.oacc[rows, :] = total
            self.gb[rows, :] = total.astype(BF)
        self.norm_back(self.after_self, 1, store)
    def back_self_a(self):
        self.weight_grad_after(self.ctx, self.gb, 3, self.ctx)
    def back_self_norm(self):
        def store(rows, dv):
            self.gb[rows, :] = (self.oacc[rows, :] + dv).astype(BF)
        self.norm_back(self.hid, 0, store)

def layer_scratch(trees):
    T = trees * TREE
    V = pltpu.VMEM
    b = lambda: V((T, SQ), BF)
    f = lambda: V((T, SQ), F32)
    d = {k: b() for k in ("ns", "q", "k", "v", "ctx", "nc", "cq", "ck", "cv", "cctx", "nf", "gb", "stage")}
    d.update({k: f() for k in ("after_self", "after_cross", "oacc", "gn")})
    d.update(ps=V((trees * H, TREE, TREE), BF), pc=V((trees * H, TREE, TREE), BF),
             mask=V((trees, TREE, TREE), F32), hot=V((trees, TREE, DEPTHS), BF), hot_t=V((trees, DEPTHS, TREE), BF),
             toep=V((H, DEPTHS, DEPTHS), BF), gains=V((16, SQ), F32), gain_grads=V((16, SQ), F32),
             bias_grads=V((128, 128), F32), inner=V((T, 512), BF), ggate=V((T, 512), BF), gup=V((T, 512), BF))
    return d


MESH = pl.DeviceIdType.MESH
TEAM_R, TEAM_S = 4, 8
NZ = TEAM_S // 2


class Team:
    def __init__(self, shard_count):
        self.fold = shard_count // TEAM_S
        r = lax.axis_index("replica")
        s = lax.axis_index("shard")
        self.base_r = (r // TEAM_R) * TEAM_R
        self.q = r % TEAM_R
        self.off_s = s % self.fold
        self.s = s // self.fold
        self.z = self.s // 2
        self.c = self.s % 2
        self.qx = self.q + 1 - 2 * (self.q % 2)
        self.qy = self.q + 2 - 4 * (self.q // 2)
        self.qd = 3 - self.q
        self.sib = self.dev(self.q, self.z * 2 + 1 - self.c)
        self.nb = (self.dev(self.qx, self.s), self.dev(self.qy, self.s))
        self.diag = self.dev(self.qd, self.s)
        self.qn = (self.qx, self.qy)

    def dev(self, q, s):
        return (self.base_r + q, s * self.fold + self.off_s)

    def zdev(self, k):
        return self.dev(self.q, ((self.z + k) % NZ) * 2 + self.c)

    def zsrc(self, k):
        return (self.z + NZ - k) % NZ


def rcopy(src, dst, send_sem, recv_sem, device):
    return pltpu.make_async_remote_copy(
        src_ref=src, dst_ref=dst, send_sem=send_sem, recv_sem=recv_sem, device_id=device, device_id_type=MESH
    )


class Sender:
    def __init__(self, team):
        self.t = team
        self.sends = {}

    def go(self, src, dst, send_sem, recv_sem, device, key=0):
        cp = rcopy(src, dst, send_sem, recv_sem, device)
        cp.start()
        self.sends.setdefault(key, []).append(cp)

    def got(self, ref, sem):
        rcopy(ref, ref, sem, sem, self.t.sib).wait_recv()

    def sent(self, key=0):
        for cp in self.sends.pop(key, ()):
            cp.wait_send()


PHASES = (("sq", 0, SQ), ("sq", 4, SQ), ("gu", 0, 1024), ("dn", 0, SQ), ("gu", 1024, 1024))


class Gather(Sender):
    def __init__(self, team, bufs, sems):
        super().__init__(team)
        self.done = [0, 0, 0]
        self.sq, self.gu, self.dn = bufs
        (self.zs, self.zr, self.xs, self.xr, self.ys, self.yr, self.dxs, self.dxr, self.dys, self.dyr, self.cs, self.cr) = sems

    def piece(self, p, q, z, half=None):
        kind, first, n = PHASES[p]
        c = self.t.c
        lo = 0 if half is None else half * (n // 2)
        w = n if half is None else n // 2
        if kind == "sq":
            ref = self.sq.at[first + q, z, c]
        elif kind == "gu":
            ref, lo = self.gu.at[q // 2, z, c, q % 2], lo + first
        else:
            ref = self.dn.at[z, c, q]
        return ref.at[:, pl.ds(lo, w)]

    def all_of(self, p, z, c):
        kind, first, n = PHASES[p]
        if kind == "sq":
            return self.sq.at[pl.ds(first, 4), z, c]
        if kind == "gu":
            return self.gu.at[:, z, c, :, :, pl.ds(first, n)]
        return self.dn.at[z, c]

    def begin(self, p):
        t = self.t
        ref = self.piece(p, t.q, t.z)
        for k in range(1, NZ):
            self.go(ref, ref, self.zs.at[p, k], self.zr.at[p, k], t.zdev(k), p)
        own = self.all_of(p, t.z, t.c)
        self.go(own, own, self.cs.at[p, 0], self.cr.at[p], t.sib, p)

    def zstep(self, p, k):
        t = self.t
        ref = self.piece(p, t.q, t.zsrc(k))
        self.got(ref, self.zr.at[p, k])
        self.go(ref, ref, self.xs.at[p, k], self.xr.at[p, k], t.nb[0], p)
        self.go(ref, ref, self.ys.at[p, k], self.yr.at[p, k], t.nb[1], p)
        self.go(ref, ref, self.cs.at[p, 5 * k - 4], self.cr.at[p], t.sib, p)

    def xystep(self, p, k):
        t = self.t
        z = t.zsrc(k)
        ref = self.piece(p, t.qx, z)
        self.got(ref, self.xr.at[p, k])
        h = self.piece(p, t.qx, z, 0)
        self.go(h, h, self.dys.at[p, k], self.dyr.at[p, k], t.nb[1], p)
        self.go(ref, ref, self.cs.at[p, 5 * k - 3], self.cr.at[p], t.sib, p)
        ref = self.piece(p, t.qy, z)
        self.got(ref, self.yr.at[p, k])
        h = self.piece(p, t.qy, z, 1)
        self.go(h, h, self.dxs.at[p, k], self.dxr.at[p, k], t.nb[0], p)
        self.go(ref, ref, self.cs.at[p, 5 * k - 2], self.cr.at[p], t.sib, p)

    def dstep(self, p, k):
        t = self.t
        z = t.zsrc(k)
        for half, sem, i in ((0, self.dyr, 1), (1, self.dxr, 0)):
            h = self.piece(p, t.qd, z, half)
            self.got(h, sem.at[p, k])
            self.go(h, h, self.cs.at[p, 5 * k - i], self.cr.at[p], t.sib, p)

    def run(self, nz, nx, nd):
        for i in range(max(self.done[0], nz)):
            for step, (what, upto) in enumerate(((self.zstep, nz), (self.xystep, nx), (self.dstep, nd))):
                n = self.done[step]
                if n < upto:
                    p, k = n // (NZ - 1), n % (NZ - 1) + 1
                    if step == 0 and k == 1 and p + 2 < len(PHASES):
                        self.begin(p + 2)
                    what(p, k)
                    self.done[step] += 1

    def whole(self, p):
        self.got(self.all_of(p, slice(None), 1 - self.t.c), self.cr.at[p])


CHUNKS = (
    ("gu", 0, 0, 48, 0, 512),
    ("gu", 0, 0, 48, 512, 512),
    ("gu", 0, 0, 48, 1024, 512),
    ("gu", 0, 0, 48, 1536, 512),
    ("dn", 0, 0, 64, 0, SQ),
    ("sq", 4, 0, 48, 0, SQ),
    ("sq", 4, 48, 48, 0, SQ),
    ("sq", 0, 0, 48, 0, SQ),
    ("sq", 0, 48, 48, 0, SQ),
)
ENTRY = (0, 1, 2, 3, 4, 6, 7, 9, 10)
KINDS = {"sq": 0, "gu": 1, "dn": 2}
ROWS = (96, 48, 64)
LAND = (SQ, 1536, SQ)
STAGES = 7


class Reduce(Sender):
    def __init__(self, team, bufs, rc, r1, r2, rz, fin, sems):
        super().__init__(team)
        self.sq, self.gu, self.dn = bufs
        self.rc, self.r1, self.r2, self.rz, self.fin = rc, r1, r2, rz, fin
        (self.s_c, self.r_c, self.s_1, self.r_1, self.s_2, self.r_2, self.s_z, self.r_z, self.s_f, self.r_f) = sems

    def rows(self, ch):
        return pl.ds(ch[2], ch[3])

    def cols(self, ch, h=None):
        if h is None:
            return pl.ds(ch[4], ch[5])
        return pl.ds(ch[4] + h * (ch[5] // 2), ch[5] // 2)

    def land(self, ch):
        return pl.ds((ch[4] % LAND[KINDS[ch[0]]]) // 2, ch[5] // 2)

    def spot(self, ch):
        return pl.ds(ch[4] % LAND[KINDS[ch[0]]], ch[5])

    def view(self, ch, q, z, c, h=None):
        kind, w = ch[0], ch[1]
        rows, cols = self.rows(ch), self.cols(ch, h)
        if kind == "sq":
            return self.sq.at[w + q, z, c, rows, cols]
        if kind == "gu":
            return self.gu.at[q // 2, z, c, q % 2, rows, cols]
        return self.dn.at[z, c, q, rows, cols]

    def half(self, ch, c):
        kind, w = ch[0], ch[1]
        rows, cols = self.rows(ch), self.cols(ch)
        if kind == "sq":
            return self.sq.at[pl.ds(w, 4), :, c, rows, cols]
        if kind == "gu":
            return self.gu.at[:, :, c, :, rows, cols]
        return self.dn.at[:, c, :, rows, cols]

    def from_core(self, ch, q=None, z=None):
        b = self.rc[KINDS[ch[0]]]
        rows, cols = self.rows(ch), self.spot(ch)
        if ch[0] == "sq":
            return b.at[:, :, rows, cols] if q is None else b.at[q, z, rows, cols]
        if ch[0] == "gu":
            return b.at[:, :, :, rows, cols] if q is None else b.at[q // 2, z, q % 2, rows, cols]
        return b.at[:, :, rows, cols] if q is None else b.at[z, q, rows, cols]

    def final(self, ch):
        return self.fin[0 if ch[1] == 0 else 1] if ch[0] == "sq" else self.fin[1 + KINDS[ch[0]]]

    def stage(self, st, i):
        t, ch = self.t, CHUNKS[i]
        q, z, c = t.q, t.z, t.c
        kd = KINDS[ch[0]]
        rows, land = self.rows(ch), self.land(ch)
        if st == 0:
            self.go(self.half(ch, 1 - c), self.from_core(ch), self.s_c.at[i], self.r_c.at[i], t.sib)
        elif st == 1:
            self.got(self.from_core(ch), self.r_c.at[i])

            @pl.loop(0, 4 * NZ)
            def _(j):
                a, b = self.view(ch, j // NZ, j % NZ, c), self.from_core(ch, j // NZ, j % NZ)
                a[...] = a[...] + b[...]

            for h in range(2):
                for m, qq in enumerate((t.qn[h], t.qd)):
                    slot = (qq // 2) if h == 0 else (qq % 2)
                    self.go(
                        self.view(ch, qq, slice(None), c, h), self.r1[kd].at[h, slot, :, rows, land],
                        self.s_1.at[i, h, m], self.r_1.at[i, h, m], t.nb[h],
                    )
        elif st == 2:
            for h in range(2):
                for m, qq in ((1, t.qn[1 - h]), (0, q)):
                    slot = (qq // 2) if h == 0 else (qq % 2)
                    self.got(self.r1[kd].at[h, slot, :, rows, land], self.r_1.at[i, h, m])

                    @pl.loop(0, NZ)
                    def _(j):
                        a = self.view(ch, qq, j, c, h)
                        a[...] = a[...] + self.r1[kd][h, slot, j, rows, land]

            for h in range(2):
                self.go(
                    self.view(ch, t.qn[1 - h], slice(None), c, h), self.r2[kd].at[h, :, rows, land],
                    self.s_2.at[i, h], self.r_2.at[i, h], t.nb[1 - h],
                )
        elif st == 3:
            for h in range(2):
                self.got(self.r2[kd].at[h, :, rows, land], self.r_2.at[i, h])

                @pl.loop(0, NZ)
                def _(j):
                    a = self.view(ch, q, j, c, h)
                    a[...] = a[...] + self.r2[kd][h, j, rows, land]

            for k in range(1, NZ):
                self.go(
                    self.view(ch, q, (z + k) % NZ, c), self.rz[kd].at[k - 1, rows, self.spot(ch)],
                    self.s_z.at[i, k], self.r_z.at[i, k], t.zdev(k),
                )
        elif st == 4:
            v = self.view(ch, q, z, c)[...].astype(F32)
            for k in range(1, NZ):
                self.got(self.rz[kd].at[k - 1, rows, self.spot(ch)], self.r_z.at[i, k])
                v = v + self.rz[kd][k - 1, rows, self.spot(ch)].astype(F32)
            f = self.final(ch).at[q, rows, self.cols(ch)]
            f[...] = v.astype(BF)
            for h in range(2):
                self.go(f, f, self.s_f.at[i, h], self.r_f.at[i, h], t.nb[h])
        elif st == 5:
            for h in range(2):
                self.got(self.final(ch).at[t.qn[h], rows, self.cols(ch)], self.r_f.at[i, h])
                f = self.final(ch).at[t.qn[h], rows, self.cols(ch, h)]
                self.go(f, f, self.s_f.at[i, 2 + h], self.r_f.at[i, 2 + h], t.nb[1 - h])
        else:
            for h in range(2):
                self.got(self.final(ch).at[t.qd, rows, self.cols(ch, h)], self.r_f.at[i, 2 + h])

    def tick(self, n):
        for st in (1, 0, 6, 5, 4, 3, 2):
            for i, entry in enumerate(ENTRY):
                if n - entry == st:
                    self.stage(st, i)


def layer_kernel(names, shards, trees, *refs):
    seg_start, seg_parent, bucket, *gains_in, bias_in, hid_in, enc_in, dy_in = refs[:10]
    weights = refs[10:21]
    lo, gh, ge, f0, f1, f2, f3, small_fin = refs[21:29]
    r = dict(zip(names, refs[29:]))
    bufs = (r["sq"], r["gu"], r["dn"])
    t = Team(shards)
    L = Layer(dict(r, seg_start=seg_start, seg_parent=seg_parent, bucket=bucket), trees)
    G = Gather(t, bufs, [r["g%d" % i] for i in range(12)])
    R = Reduce(
        t, bufs, [r["rc0"], r["rc1"], r["rc2"]], [r["ra0"], r["ra1"], r["ra2"]], [r["rb0"], r["rb1"], r["rb2"]],
        [r["rz0"], r["rz1"], r["rz2"]], (f0, f1, f2, f3), [r["r%d" % i] for i in range(10)],
    )
    S = Sender(t)

    loc, lsem = [], r["local"]

    def fetch(src, dst):
        cp = pltpu.make_async_copy(src, dst, lsem.at[len(loc)])
        cp.start()
        loc.append(cp)

    z, c = t.z, t.c
    for i in range(8):
        fetch(weights[i], r["sq"].at[i, z, c])
    for i in range(2):
        for h in range(2):
            fetch(weights[8 + i].at[pl.ds(h * 48, 48)], r["gu"].at[i, z, c, h])
    for h in range(4):
        fetch(weights[10].at[pl.ds(h * 64, 64)], r["dn"].at[z, c, h])
    fetch(hid_in, r["hid"])
    fetch(enc_in, r["enc"])
    fetch(dy_in, r["dy"])

    others = [t.dev(t.q, (t.s + k) % TEAM_S) for k in range(1, TEAM_S)]
    greet = others + list(t.nb) + [t.diag]
    barrier = pltpu.get_barrier_semaphore()
    for d in greet:
        pl.semaphore_signal(barrier, inc=1, device_id=d, device_id_type=MESH)
    pl.semaphore_wait(barrier, len(greet))
    for cp in loc:
        cp.wait()

    small, mix = r["small"], r["mix"]
    mix[...] = jnp.zeros_like(mix)
    for i in range(3):
        mix[i:i + 1, :96] = gains_in[i][...].astype(F32)
    mix[4:8, :H] = bias_in[...].astype(F32)
    small[t.s] = mix[...].astype(BF)
    for k in range(1, TEAM_S):
        S.go(small.at[t.s], small.at[t.s], r["ss"].at[0, k], r["sr"].at[0, k], others[k - 1])
    G.begin(0)
    G.begin(1)
    L.layout()
    G.run(1, 0, 0)
    for k in range(1, TEAM_S):
        S.got(small.at[(t.s + TEAM_S - k) % TEAM_S], r["sr"].at[0, k])
    L.small_params()
    G.run(2, 1, 0)
    L.norm(r["hid"], r["ns"], 0)
    G.run(3, 2, 1)
    G.run(4, 3, 2)
    G.run(5, 4, 3)
    G.run(6, 4, 3)
    own = (r["q"], r["k"], r["v"], r["ctx"], r["ps"], True)
    cross = (r["cq"], r["ck"], r["cv"], r["cctx"], r["pc"], False)
    G.whole(0)
    for w in range(3):
        L.project(r["ns"], w, own[w])
    for n in range(4):
        G.run(7 + n, 5 + n, 3 + n)
        L.attend(*own, 3 * n, 3 * n + 3)
    G.run(11, 9, 7)
    L.project_add(r["ctx"], 3, r["hid"], r["after_self"])
    L.norm(r["after_self"], r["nc"], 1)
    G.whole(1)
    L.project(r["nc"], 4, r["cq"])
    G.run(12, 10, 8)
    L.project(r["enc"], 5, r["ck"])
    L.project(r["enc"], 6, r["cv"])
    L.attend(*cross, 0, 3)
    G.run(13, 11, 9)
    L.attend(*cross, 3, 9)
    G.run(14, 12, 10)
    L.attend(*cross, 9, 12)
    L.project_add(r["cctx"], 7, r["after_self"], r["after_cross"])
    G.run(15, 13, 11)
    L.start_ff()
    G.run(15, 14, 12)
    for p in (2, 3):
        G.whole(p)
    G.run(15, 15, 13)
    for p in (2, 3):
        G.sent(p)

    L.feed_forward(0)
    G.run(15, 15, 15)
    R.tick(0)
    L.feed_forward(1)
    R.tick(1)
    G.whole(4)
    for p in (4, 0, 1):
        G.sent(p)
    S.sent()
    for m in (2, 3):
        L.feed_forward(m)
        R.tick(m)
    L.end_ff()
    out0 = pltpu.make_async_copy(r["stage"], lo, lsem.at[0])
    out0.start()
    L.back_ff_norm()
    out0.wait()
    L.back_cross_a()
    R.tick(4)
    L.attend_back(*cross, 0, 6)
    R.tick(5)
    L.attend_back(*cross, 6, 12)
    L.back([(r["ck"], 5), (r["cv"], 6)], r["stage"], BF)
    out1 = pltpu.make_async_copy(r["stage"], ge, lsem.at[1])
    out1.start()
    L.back([(r["cq"], 4)], r["gn"], F32)
    L.weight_grad(r["nc"], r["cq"], 4)
    L.weight_grad(r["enc"], r["ck"], 5)
    L.weight_grad(r["enc"], r["cv"], 6)
    R.tick(6)
    L.back_cross_norm()
    out1.wait()
    L.back_self_a()
    L.attend_back(*own, 0, 3)
    R.tick(7)
    L.attend_back(*own, 3, 9)
    R.tick(8)
    L.attend_back(*own, 9, 12)
    L.back([(r["q"], 0), (r["k"], 1), (r["v"], 2)], r["gn"], F32)
    L.weight_grad(r["ns"], r["q"], 0)
    L.weight_grad(r["ns"], r["k"], 1)
    L.weight_grad(r["ns"], r["v"], 2)
    R.tick(9)
    L.back_self_norm()
    out2 = pltpu.make_async_copy(r["gb"], gh, lsem.at[2])
    out2.start()
    L.small_grads()
    so, sa, sb = r["small_out"], r["small_a"], r["small_b"]
    for k in range(1, TEAM_S):
        S.go(so.at[(t.s + k) % TEAM_S], sa.at[t.s], r["ss"].at[1, k], r["sr"].at[1, k], others[k - 1])
    sa[t.s] = so[t.s]
    R.tick(10)
    for k in range(1, TEAM_S):
        S.got(sa.at[(t.s + TEAM_S - k) % TEAM_S], r["sr"].at[1, k])
    sb[t.q] = jnp.sum(sa[...].astype(F32), axis=0).astype(BF)
    for k, (qq, d) in enumerate(((t.qx, t.nb[0]), (t.qy, t.nb[1]), (t.qd, t.diag))):
        S.go(sb.at[t.q], sb.at[t.q], r["ss"].at[2, k], r["sr"].at[2, k], d)
    last = max(ENTRY) + STAGES
    R.tick(11)
    for k, qq in enumerate((t.qx, t.qy, t.qd)):
        S.got(sb.at[qq], r["sr"].at[2, k])
    small_fin[...] = jnp.sum(sb[...].astype(F32), axis=0)
    for n in range(12, last):
        R.tick(n)
    R.sent()
    S.sent()
    out2.wait()


def layer(seg_start, seg_parent, bucket, gains, bias, hid, enc, dy, weights, shards):
    trees = seg_start.shape[0]
    tokens = trees * TREE
    V, D = pltpu.VMEM, pltpu.SemaphoreType.DMA
    act = lambda: V((tokens, SQ), BF)
    n, p = len(CHUNKS), len(PHASES)
    scratch = dict(
        sq=V((8, NZ, 2, 96, SQ), BF), gu=V((2, NZ, 2, 2, 48, FFN), BF), dn=V((NZ, 2, 4, 64, SQ), BF),
        rc0=V((4, NZ, 96, SQ), BF), rc1=V((2, NZ, 2, 48, LAND[1]), BF), rc2=V((NZ, 4, 64, SQ), BF),
        hid=act(), enc=act(), dy=act(), local=D((20,)),
        small=V((8, 16, 128), BF), small_out=V((8, 16, 128), BF), small_a=V((8, 16, 128), BF), small_b=V((4, 16, 128), BF),
        ss=D((3, 8)), sr=D((3, 8)), mix=V((16, 128), F32),
    )
    for i in range(3):
        scratch["ra%d" % i] = V((2, 2, NZ, ROWS[i], LAND[i] // 2), BF)
        scratch["rb%d" % i] = V((2, NZ, ROWS[i], LAND[i] // 2), BF)
        scratch["rz%d" % i] = V((NZ - 1, ROWS[i], LAND[i]), BF)
    for i in range(12):
        scratch["g%d" % i] = D((p, 16)) if i == 10 else D((p,)) if i == 11 else D((p, NZ))
    for i, shape in enumerate([(n,), (n,), (n, 2, 2), (n, 2, 2), (n, 2), (n, 2), (n, NZ), (n, NZ), (n, 4), (n, 4)]):
        scratch["r%d" % i] = D(shape)
    scratch.update(layer_scratch(trees))
    hbm, vmem, smem = (pl.BlockSpec(memory_space=m) for m in (pltpu.HBM, pltpu.VMEM, pltpu.SMEM))
    sd = jax.ShapeDtypeStruct
    return pl.pallas_call(
        functools.partial(layer_kernel, list(scratch), shards, trees),
        out_shape=[sd((tokens, SQ), BF)] * 3
        + [sd((4, 96, SQ), BF), sd((4, 96, SQ), BF), sd((4, 48, FFN), BF), sd((4, 64, SQ), BF), sd((16, 128), F32)],
        in_specs=[smem, smem] + [vmem] * 5 + [hbm] * 14,
        out_specs=[hbm] * 3 + [vmem] * 5,
        scratch_shapes=list(scratch.values()),
        compiler_params=pltpu.CompilerParams(collective_id=0, has_side_effects=True, vmem_limit_bytes=64 * 2**20 - 65536),
        name="decoder_layer",
    )(seg_start, seg_parent, bucket, *gains, bias, hid, enc, dy, *weights)


def finish_kernel(lo, gh, ge, f0, f1, f2, f3, small, *refs):
    o_lo, o_gh, o_ge = refs[:3]
    squares, gate, up, down = refs[3:11], refs[11], refs[12], refs[13]
    norms, table = refs[14:17], refs[17]
    a0, a1, a2, b0, b1, b2, b3, w0, w1, w2, w3, sem_in, sem_out = refs[18:]
    pairs = ((f0, b0), (f1, b1), (f2, b2), (f3, b3), (lo, a0), (gh, a1), (ge, a2))
    ins = [pltpu.make_async_copy(a, b, sem_in.at[i]) for i, (a, b) in enumerate(pairs)]
    for cp in ins:
        cp.start()
    for i in range(3):
        norms[i][...] = small[i:i + 1, :96]
    table[...] = small[4:8, :H]
    outs = []

    def out(src, dst):
        cp = pltpu.make_async_copy(src, dst, sem_out.at[len(outs)])
        cp.start()
        outs.append(cp)

    for n, (b, w) in enumerate(((b0, w0), (b1, w1))):
        ins[n].wait()
        for i in range(4):
            w[i] = b[i].astype(F32)
            out(w.at[i], squares[4 * n + i])
    ins[2].wait()
    for i, dst in enumerate((gate, up)):
        w2[i] = b2[2 * i:2 * i + 2].reshape(96, FFN).astype(F32)
        out(w2.at[i], dst)
    ins[3].wait()
    w3[...] = b3[...].reshape(256, SQ).astype(F32)
    out(w3, down)
    for i, dst in enumerate((o_lo, o_gh, o_ge)):
        ins[4 + i].wait()
        out((a0, a1, a2)[i], dst)
    for cp in outs:
        cp.wait()


def finish(outs):
    hbm, vmem = pl.BlockSpec(memory_space=pltpu.HBM), pl.BlockSpec(memory_space=pltpu.VMEM)
    V, sd = pltpu.VMEM, jax.ShapeDtypeStruct
    res = pl.pallas_call(
        finish_kernel,
        out_shape=[sd(o.shape, BF) for o in outs[:3]] + [sd((96, SQ), F32)] * 8 + [sd((96, FFN), F32)] * 2
        + [sd((256, SQ), F32)] + [sd((1, 96), F32)] * 3 + [sd((4, H), F32)],
        in_specs=[hbm] * 7 + [vmem],
        out_specs=[hbm] * 14 + [vmem] * 4,
        scratch_shapes=[V(o.shape, BF) for o in outs[:7]]
        + [V((4, 96, SQ), F32), V((4, 96, SQ), F32), V((2, 96, FFN), F32), V((256, SQ), F32)]
        + [pltpu.SemaphoreType.DMA((7,)), pltpu.SemaphoreType.DMA((14,))],
        compiler_params=pltpu.CompilerParams(vmem_limit_bytes=63 * 2**20),
        name="finish",
    )(*outs)
    return (*res[:3], res[3:11], res[11], res[12], res[13], res[14:17], res[17])


def team_rows(weight, fold):
    if fold == 1:
        return weight
    groups = [[a * fold + b for b in range(fold)] for a in range(TEAM_S)]
    return lax.all_gather(weight, "shard", axis=0, tiled=True, axis_index_groups=groups)


def team_sum(grad, fold, teams_r):
    if fold > 1:
        groups = [[a * fold + b for b in range(fold)] for a in range(TEAM_S)]
        grad = lax.psum_scatter(grad, "shard", scatter_dimension=0, tiled=True, axis_index_groups=groups)
    if teams_r > 1:
        groups = [[a * TEAM_R + b for a in range(teams_r)] for b in range(TEAM_R)]
        grad = lax.psum(grad, "replica", axis_index_groups=groups)
    return grad


def body(
    replicas, shards,
    hidden, encoded, out_grad, seg_start, seg_parent, bucket_of_distance,
    norm_self, self_query, self_key, self_value, self_out, rel_bias,
    norm_cross, cross_query, cross_key, cross_value, cross_out,
    norm_ff, ff_gate, ff_up, ff_down,
):
    fold, teams_r = shards // TEAM_S, replicas // TEAM_R
    big = (self_query, self_key, self_value, self_out, cross_query, cross_key, cross_value, cross_out, ff_gate, ff_up, ff_down)
    flat = lambda v: v.reshape(-1, v.shape[-1])
    outs = layer(
        flat(seg_start), flat(seg_parent), bucket_of_distance.reshape(2, 128),
        [team_rows(g, fold).reshape(1, -1) for g in (norm_self, norm_cross, norm_ff)], team_rows(rel_bias, fold),
        flat(hidden), flat(encoded), flat(out_grad), [team_rows(w, fold) for w in big], shards,
    )
    lo, gh, ge, squares, gate, up, down, norms, table = finish(outs)
    squares = [team_sum(v, fold, teams_r) for v in squares]
    gate, up, down, table = (team_sum(v, fold, teams_r) for v in (gate, up, down, table))
    norms = [team_sum(v.reshape(-1), fold, teams_r) for v in norms]
    lo, gh, ge = (v.reshape(hidden.shape) for v in (lo, gh, ge))
    return (
        lo, gh, ge, norms[0], *squares[:4], table, norms[1], *squares[4:], norms[2], gate, up, down,
    )


def solution(mesh):
    placed = (
        P(None, ("replica", "shard"), None, None),
        P(None, ("replica", "shard"), None, None),
        P(None, ("replica", "shard"), None, None),
        P(None, ("replica", "shard"), None),
        P(None, ("replica", "shard"), None),
        P(),
        P("shard"),
        P("shard", None),
        P("shard", None),
        P("shard", None),
        P("shard", None),
        P("shard", None),
        P("shard"),
        P("shard", None),
        P("shard", None),
        P("shard", None),
        P("shard", None),
        P("shard"),
        P("shard", None),
        P("shard", None),
        P("shard", None),
    )
    return jax.shard_map(
        functools.partial(body, mesh.shape["replica"], mesh.shape["shard"]),
        mesh=mesh,
        in_specs=placed,
        out_specs=(
            P(None, ("replica", "shard"), None, None),
            P(None, ("replica", "shard"), None, None),
            P(None, ("replica", "shard"), None, None),
            P("shard"),
            P("shard", None),
            P("shard", None),
            P("shard", None),
            P("shard", None),
            P("shard", None),
            P("shard"),
            P("shard", None),
            P("shard", None),
            P("shard", None),
            P("shard", None),
            P("shard"),
            P("shard", None),
            P("shard", None),
            P("shard", None),
        ),
        check_vma=False,
    )
```

profile of v0, /device:TPU:0, one launch (start us, length us, event | category | flops | bytes accessed | tf_op | source)
XLA Modules:
  0.0 216.2 jit_solution(2814623982145053358)
XLA Ops:
  0.7 209.8 %decoder_layer.1 = (bf16[512,768]{1,0:T(8,128)(2,1)}, bf16[512,768]{1,0:T(8,128)(2,1)}, bf16[512,768]{1,0:T(8,128)(2,1)}, bf16[4,96,768]{2,1,0:T(8,128)(2,1)}, b...) custom-call(s32[2,13]{1,0:T(2,128)} %bitcast.24, ...), custom_call_target="tpu_custom_call" | custom-call | tf_op jit(solution)/shard_map/decoder_layer/pallas_call | solution.py:765
  210.5 5.5 %finish.1 = (bf16[512,768]{1,0:T(8,128)(2,1)}, bf16[512,768]{1,0:T(8,128)(2,1)}, bf16[512,768]{1,0:T(8,128)(2,1)}, f32[96,768]{1,0:T(8,128)}, f32[96,768]{1,0:T(...) custom-call(bf16[512,768]{1,0:T(8,128)(2,1)} %get-tuple-element.44.l, ...), custom_call_target="tpu_custom_call" | custom-call | tf_op jit(solution)/shard_map/finish/pallas_call | solution.py:818
where the time goes:
time: 218 us; the launch traced here: 216 us
  Pallas kernels  215 us (99%)
    pallas_call x1, Pallas kernels, layer(): pl.pallas_call(functools.partial(layer_kernel, list(scratch), shards, tre...  210 us
    pallas_call x1, Pallas kernels, finish(): pl.pallas_call(finish_kernel, out_shape=[sd(o.shape, BF) for o in outs[:3...  5.49 us

commit v1 on v0

--- a/solution.py
+++ b/solution.py
@@ -104,8 +104,8 @@
             store(rows, r * (dg - n * jnp.mean(dg * n, axis=-1, keepdims=True)))
 
     def wsq(self, w): return self.sq[w].reshape(SQ, SQ)
-    def project(self, src, w, dst):
-        @pl.loop(0, 3, unroll=3)
+    def project(self, src, w, dst, first=0, last=3):
+        @pl.loop(first, last, unroll=last - first)
         def _(n):
             cols = pl.ds(pl.multiple_of(n * 256, 256), 256)
             wt = self.sq[w, :, :, :, cols].reshape(SQ, 256)
@@ -143,54 +143,78 @@
     def lanes(self):
         low = lax.broadcasted_iota(jnp.int32, (TREE, 128), 1) < DH
         return low, jnp.logical_not(low)
+    def block(self, n):
+        rows, cols = slice((n % 2) * TREE, (n % 2) * TREE + TREE), slice((n // 2) * TREE, (n // 2) * TREE + TREE)
+        return self.gn.at[rows, cols]
     def attend(self, q, k, v, ctx, probs, masked, first, last):
         halves = self.lanes()
-        @pl.loop(first * self.trees // 2, last * self.trees // 2, unroll=3)
-        def _(i):
-            t, p = i // (H // 2), i % (H // 2)
-            rows = pl.ds(pl.multiple_of(t * TREE, TREE), TREE)
-            cols = pl.ds(pl.multiple_of(p * 128, 128), 128)
-            qp, kp, vt = q[rows, cols], k[rows, cols], v[rows, cols].T
-            if masked:
-                hot = self.hot[t]
-                kp = jnp.concatenate([kp, hot], axis=1)
-            outs = []
-            for e in range(2):
-                qe = jnp.where(halves[e], qp, jnp.zeros_like(qp))
+        @pl.loop(first * self.trees // 6, last * self.trees // 6)
+        def _(n):
+            def place(u):
+                i = n * 3 + u
+                t, p = i % self.trees, i // self.trees
+                return t, p, pl.ds(pl.multiple_of(t * TREE, TREE), TREE), pl.ds(pl.multiple_of(p * 128, 128), 128)
+            for u in range(3):
+                t, p, rows, cols = place(u)
+                qp, kp = q[rows, cols], k[rows, cols]
                 if masked:
-                    qe = jnp.concatenate([qe, nt(hot, self.toep[2 * p + e]).astype(BF)], axis=1)
-                s = nt(kp, qe)
-                if masked:
-                    s = s + self.mask[t]
-                x = jnp.exp(s - jnp.max(s, axis=0, keepdims=True))
-                pr = (x * (1.0 / jnp.sum(x, axis=0, keepdims=True))).astype(BF)
-                probs[2 * i + e] = pr
-                outs.append(nn(vt[e * DH:(e + 1) * DH], pr))
-            ctx[rows, cols] = jnp.concatenate(outs, axis=0).astype(BF).T
+                    hot = self.hot[t]
+                    kp = jnp.concatenate([kp, hot], axis=1)
+                for e in range(2):
+                    qe = jnp.where(halves[e], qp, jnp.zeros_like(qp))
+                    if masked:
+                        qe = jnp.concatenate([qe, nt(hot, self.toep[2 * p + e]).astype(BF)], axis=1)
+                    self.block(2 * u + e)[...] = nt(kp, qe)
+            for u in range(3):
+                t, p, rows, cols = place(u)
+                for e in range(2):
+                    s = self.block(2 * u + e)[...]
+                    if masked:
+                        s = s + self.mask[t]
+                    x = jnp.exp(s - jnp.max(s, axis=0, keepdims=True))
+                    probs[t * H + 2 * p + e] = (x * (1.0 / jnp.sum(x, axis=0, keepdims=True))).astype(BF)
+            for u in range(3):
+                t, p, rows, cols = place(u)
+                vt = v[rows, cols].T
+                outs = [nn(vt[e * DH:(e + 1) * DH], probs[t * H + 2 * p + e]) for e in range(2)]
+                ctx[rows, cols] = jnp.concatenate(outs, axis=0).astype(BF).T
     def attend_back(self, q, k, v, dctx, probs, masked, first, last):
         halves = self.lanes()
-        @pl.loop(first * self.trees // 2, last * self.trees // 2, unroll=3)
-        def _(i):
-            t, p = i // (H // 2), i % (H // 2)
-            rows = pl.ds(pl.multiple_of(t * TREE, TREE), TREE)
-            cols = pl.ds(pl.multiple_of(p * 128, 128), 128)
-            qp, kt, vp, dp = q[rows, cols], k[rows, cols].T, v[rows, cols], dctx[rows, cols]
-            dq, dk, dv = [], [], []
-            for e in range(2):
-                pr = probs[2 * i + e]
-                prf = pr.astype(F32)
-                g = nt(vp, jnp.where(halves[e], dp, jnp.zeros_like(dp)))
-                ds = (prf * (g - jnp.sum(g * prf, axis=0, keepdims=True))).astype(BF)
-                dv.append(nn(pr, dp))
-                dq.append(nn(kt[e * DH:(e + 1) * DH], ds))
-                dk.append(nn(ds, qp))
-                if masked:
-                    m = nn(nn(self.hot_t[t], ds).astype(BF), self.hot[t])
-                    m = pltpu.roll(m, 1, 1, stride=1, stride_axis=0)
-                    self.bias_grads[pl.ds(2 * p + e, 1), :] += jnp.sum(m, axis=0, keepdims=True)
-            q[rows, cols] = jnp.concatenate(dq, axis=0).astype(BF).T
-            k[rows, cols] = jnp.where(halves[0], dk[0], dk[1]).astype(BF)
-            v[rows, cols] = jnp.where(halves[0], dv[0], dv[1]).astype(BF)
+        @pl.loop(first * self.trees // 6, last * self.trees // 6)
+        def _(n):
+            def place(u):
+                i = n * 3 + u
+                t, p = i % self.trees, i // self.trees
+                return t, p, pl.ds(pl.multiple_of(t * TREE, TREE), TREE), pl.ds(pl.multiple_of(p * 128, 128), 128)
+            for u in range(3):
+                t, p, rows, cols = place(u)
+                vp, dp = v[rows, cols], dctx[rows, cols]
+                dv = []
+                for e in range(2):
+                    self.block(2 * u + e)[...] = nt(vp, jnp.where(halves[e], dp, jnp.zeros_like(dp)))
+                    dv.append(nn(probs[t * H + 2 * p + e], dp))
+                v[rows, cols] = jnp.where(halves[0], dv[0], dv[1]).astype(BF)
+            for u in range(3):
+                t, p, rows, cols = place(u)
+                for e in range(2):
+                    g = self.block(2 * u + e)[...]
+                    prf = probs[t * H + 2 * p + e].astype(F32)
+                    ds = prf * (g - jnp.sum(g * prf, axis=0, keepdims=True))
+                    probs[t * H + 2 * p + e] = ds.astype(BF)
+            for u in range(3):
+                t, p, rows, cols = place(u)
+                qp, kt = q[rows, cols], k[rows, cols].T
+                dq, dk = [], []
+                for e in range(2):
+                    ds = probs[t * H + 2 * p + e]
+                    dq.append(nn(kt[e * DH:(e + 1) * DH], ds))
+                    dk.append(nn(ds, qp))
+                    if masked:
+                        m = nn(nn(self.hot_t[t], ds).astype(BF), self.hot[t])
+                        m = pltpu.roll(m, 1, 1, stride=1, stride_axis=0)
+                        self.bias_grads[pl.ds(2 * p + e, 1), :] += jnp.sum(m, axis=0, keepdims=True)
+                q[rows, cols] = jnp.concatenate(dq, axis=0).astype(BF).T
+                k[rows, cols] = jnp.where(halves[0], dk[0], dk[1]).astype(BF)
 
     def feed_forward(self, m):
         base = pl.multiple_of(m * 512, 512)
@@ -344,7 +368,10 @@
             cp.wait_send()
 
 
-PHASES = (("sq", 0, SQ), ("sq", 4, SQ), ("gu", 0, 1024), ("dn", 0, SQ), ("gu", 1024, 1024))
+PHASES = (
+    ("sq", 0, 0, 256), ("sq", 0, 256, 512), ("sq", 4, 0, SQ), ("gu", 0, 0, 1024), ("dn", 0, 0, SQ), ("gu", 0, 1024, 1024),
+)
+AHEAD = 1
 
 
 class Gather(Sender):
@@ -355,25 +382,26 @@
         (self.zs, self.zr, self.xs, self.xr, self.ys, self.yr, self.dxs, self.dxr, self.dys, self.dyr, self.cs, self.cr) = sems
 
     def piece(self, p, q, z, half=None):
-        kind, first, n = PHASES[p]
+        kind, first, col, n = PHASES[p]
         c = self.t.c
-        lo = 0 if half is None else half * (n // 2)
+        lo = col if half is None else col + half * (n // 2)
         w = n if half is None else n // 2
         if kind == "sq":
             ref = self.sq.at[first + q, z, c]
         elif kind == "gu":
-            ref, lo = self.gu.at[q // 2, z, c, q % 2], lo + first
+            ref = self.gu.at[q // 2, z, c, q % 2]
         else:
             ref = self.dn.at[z, c, q]
         return ref.at[:, pl.ds(lo, w)]
 
     def all_of(self, p, z, c):
-        kind, first, n = PHASES[p]
+        kind, first, col, n = PHASES[p]
+        cols = pl.ds(col, n)
         if kind == "sq":
-            return self.sq.at[pl.ds(first, 4), z, c]
+            return self.sq.at[pl.ds(first, 4), z, c, :, cols]
         if kind == "gu":
-            return self.gu.at[:, z, c, :, :, pl.ds(first, n)]
-        return self.dn.at[z, c]
+            return self.gu.at[:, z, c, :, :, cols]
+        return self.dn.at[z, c, :, :, cols]
 
     def begin(self, p):
         t = self.t
@@ -419,10 +447,10 @@
                 n = self.done[step]
                 if n < upto:
                     p, k = n // (NZ - 1), n % (NZ - 1) + 1
-                    if step == 0 and k == 1 and p + 2 < len(PHASES):
-                        self.begin(p + 2)
                     what(p, k)
                     self.done[step] += 1
+                    if step == 0 and k == 1 and p + AHEAD < len(PHASES):
+                        self.begin(p + AHEAD)
 
     def whole(self, p):
         self.got(self.all_of(p, slice(None), 1 - self.t.c), self.cr.at[p])
@@ -439,7 +467,7 @@
     ("sq", 0, 0, 48, 0, SQ),
     ("sq", 0, 48, 48, 0, SQ),
 )
-ENTRY = (0, 1, 2, 3, 4, 6, 7, 9, 10)
+ENTRY = (0, 2, 3, 4, 5, 7, 8, 10, 11)
 KINDS = {"sq": 0, "gu": 1, "dn": 2}
 ROWS = (96, 48, 64)
 LAND = (SQ, 1536, SQ)
@@ -625,8 +653,8 @@
     small[t.s] = mix[...].astype(BF)
     for k in range(1, TEAM_S):
         S.go(small.at[t.s], small.at[t.s], r["ss"].at[0, k], r["sr"].at[0, k], others[k - 1])
-    G.begin(0)
-    G.begin(1)
+    for p in range(AHEAD):
+        G.begin(p)
     L.layout()
     G.run(1, 0, 0)
     for k in range(1, TEAM_S):
@@ -637,59 +665,67 @@
     G.run(3, 2, 1)
     G.run(4, 3, 2)
     G.run(5, 4, 3)
-    G.run(6, 4, 3)
     own = (r["q"], r["k"], r["v"], r["ctx"], r["ps"], True)
     cross = (r["cq"], r["ck"], r["cv"], r["cctx"], r["pc"], False)
     G.whole(0)
     for w in range(3):
-        L.project(r["ns"], w, own[w])
-    for n in range(4):
-        G.run(7 + n, 5 + n, 3 + n)
-        L.attend(*own, 3 * n, 3 * n + 3)
+        L.project(r["ns"], w, own[w], 0, 1)
+    G.run(6, 5, 4)
+    L.attend(*own, 0, 3)
+    G.run(7, 6, 5)
+    G.run(8, 7, 6)
+    G.run(9, 7, 6)
+    G.whole(1)
+    for w in range(3):
+        L.project(r["ns"], w, own[w], 1, 3)
+    L.attend(*own, 3, 6)
+    G.run(10, 8, 6)
+    L.attend(*own, 6, 12)
     G.run(11, 9, 7)
     L.project_add(r["ctx"], 3, r["hid"], r["after_self"])
     L.norm(r["after_self"], r["nc"], 1)
-    G.whole(1)
-    L.project(r["nc"], 4, r["cq"])
     G.run(12, 10, 8)
-    L.project(r["enc"], 5, r["ck"])
-    L.project(r["enc"], 6, r["cv"])
-    L.attend(*cross, 0, 3)
     G.run(13, 11, 9)
-    L.attend(*cross, 3, 9)
+    G.whole(2)
+    for w, src in enumerate((r["nc"], r["enc"], r["enc"])):
+        L.project(src, 4 + w, cross[w])
     G.run(14, 12, 10)
-    L.attend(*cross, 9, 12)
+    L.attend(*cross, 0, 6)
+    G.run(15, 13, 11)
+    L.attend(*cross, 6, 12)
+    G.run(16, 14, 12)
     L.project_add(r["cctx"], 7, r["after_self"], r["after_cross"])
-    G.run(15, 13, 11)
     L.start_ff()
-    G.run(15, 14, 12)
-    for p in (2, 3):
+    G.run(17, 15, 13)
+    G.run(18, 16, 14)
+    G.run(18, 17, 15)
+    for p in (3, 4):
         G.whole(p)
-    G.run(15, 15, 13)
-    for p in (2, 3):
         G.sent(p)
 
     L.feed_forward(0)
-    G.run(15, 15, 15)
+    G.run(18, 18, 17)
     R.tick(0)
+    G.run(18, 18, 18)
+    R.tick(1)
     L.feed_forward(1)
-    R.tick(1)
-    G.whole(4)
-    for p in (4, 0, 1):
+    R.tick(2)
+    G.whole(5)
+    for p in (5, 0, 1, 2):
         G.sent(p)
     S.sent()
     for m in (2, 3):
         L.feed_forward(m)
-        R.tick(m)
+        R.tick(m + 1)
     L.end_ff()
     out0 = pltpu.make_async_copy(r["stage"], lo, lsem.at[0])
     out0.start()
     L.back_ff_norm()
     out0.wait()
     L.back_cross_a()
-    R.tick(4)
+    R.tick(5)
     L.attend_back(*cross, 0, 6)
-    R.tick(5)
+    R.tick(6)
     L.attend_back(*cross, 6, 12)
     L.back([(r["ck"], 5), (r["cv"], 6)], r["stage"], BF)
     out1 = pltpu.make_async_copy(r["stage"], ge, lsem.at[1])
@@ -698,20 +734,20 @@
     L.weight_grad(r["nc"], r["cq"], 4)
     L.weight_grad(r["enc"], r["ck"], 5)
     L.weight_grad(r["enc"], r["cv"], 6)
-    R.tick(6)
+    R.tick(7)
     L.back_cross_norm()
     out1.wait()
     L.back_self_a()
     L.attend_back(*own, 0, 3)
-    R.tick(7)
+    R.tick(8)
     L.attend_back(*own, 3, 9)
-    R.tick(8)
+    R.tick(9)
     L.attend_back(*own, 9, 12)
     L.back([(r["q"], 0), (r["k"], 1), (r["v"], 2)], r["gn"], F32)
     L.weight_grad(r["ns"], r["q"], 0)
     L.weight_grad(r["ns"], r["k"], 1)
     L.weight_grad(r["ns"], r["v"], 2)
-    R.tick(9)
+    R.tick(10)
     L.back_self_norm()
     out2 = pltpu.make_async_copy(r["gb"], gh, lsem.at[2])
     out2.start()
@@ -720,18 +756,18 @@
     for k in range(1, TEAM_S):
         S.go(so.at[(t.s + k) % TEAM_S], sa.at[t.s], r["ss"].at[1, k], r["sr"].at[1, k], others[k - 1])
     sa[t.s] = so[t.s]
-    R.tick(10)
+    R.tick(11)
     for k in range(1, TEAM_S):
         S.got(sa.at[(t.s + TEAM_S - k) % TEAM_S], r["sr"].at[1, k])
     sb[t.q] = jnp.sum(sa[...].astype(F32), axis=0).astype(BF)
     for k, (qq, d) in enumerate(((t.qx, t.nb[0]), (t.qy, t.nb[1]), (t.qd, t.diag))):
         S.go(sb.at[t.q], sb.at[t.q], r["ss"].at[2, k], r["sr"].at[2, k], d)
     last = max(ENTRY) + STAGES
-    R.tick(11)
+    R.tick(12)
     for k, qq in enumerate((t.qx, t.qy, t.qd)):
         S.got(sb.at[qq], r["sr"].at[2, k])
     small_fin[...] = jnp.sum(sb[...].astype(F32), axis=0)
-    for n in range(12, last):
+    for n in range(13, last):
         R.tick(n)
     R.sent()
     S.sent()

time: 218 us -> 215 us (0.986)
  Pallas kernels: 215 us -> 211 us
    pallas_call x1, Pallas kernels: 210 us -> 205 us  [layer(): pl.pallas_call(functools.partial(layer_kernel, list(scratch), shards, tre...]
where the time goes in v1:
time: 215 us; the launch traced here: 212 us
  Pallas kernels  211 us (98%)
    pallas_call x1, Pallas kernels, layer(): pl.pallas_call(functools.partial(layer_kernel, list(scratch), shards, tre...  205 us
    pallas_call x1, Pallas kernels, finish(): pl.pallas_call(finish_kernel, out_shape=[sd(o.shape, BF) for o in outs[:3...  5.49 us

profile of v1, /device:TPU:0, one launch (start us, length us, event | category | flops | bytes accessed | tf_op | source)
XLA Modules:
  0.0 211.7 jit_solution(13325361707652352307)
XLA Ops:
  0.7 205.3 %decoder_layer.1 = (bf16[512,768]{1,0:T(8,128)(2,1)}, bf16[512,768]{1,0:T(8,128)(2,1)}, bf16[512,768]{1,0:T(8,128)(2,1)}, bf16[4,96,768]{2,1,0:T(8,128)(2,1)}, b...) custom-call(s32[2,13]{1,0:T(2,128)} %bitcast.24, ...), custom_call_target="tpu_custom_call" | custom-call | tf_op jit(solution)/shard_map/decoder_layer/pallas_call | solution.py:801
  206.0 5.5 %finish.1 = (bf16[512,768]{1,0:T(8,128)(2,1)}, bf16[512,768]{1,0:T(8,128)(2,1)}, bf16[512,768]{1,0:T(8,128)(2,1)}, f32[96,768]{1,0:T(8,128)}, f32[96,768]{1,0:T(...) custom-call(bf16[512,768]{1,0:T(8,128)(2,1)} %get-tuple-element.44.l, ...), custom_call_target="tpu_custom_call" | custom-call | tf_op jit(solution)/shard_map/finish/pallas_call | solution.py:854

commit v2 on v1

--- a/solution.py
+++ b/solution.py
@@ -535,7 +535,7 @@
         elif st == 1:
             self.got(self.from_core(ch), self.r_c.at[i])
 
-            @pl.loop(0, 4 * NZ)
+            @pl.loop(0, 4 * NZ, unroll=4)
             def _(j):
                 a, b = self.view(ch, j // NZ, j % NZ, c), self.from_core(ch, j // NZ, j % NZ)
                 a[...] = a[...] + b[...]
@@ -553,7 +553,7 @@
                     slot = (qq // 2) if h == 0 else (qq % 2)
                     self.got(self.r1[kd].at[h, slot, :, rows, land], self.r_1.at[i, h, m])
 
-                    @pl.loop(0, NZ)
+                    @pl.loop(0, NZ, unroll=NZ)
                     def _(j):
                         a = self.view(ch, qq, j, c, h)
                         a[...] = a[...] + self.r1[kd][h, slot, j, rows, land]
@@ -567,7 +567,7 @@
             for h in range(2):
                 self.got(self.r2[kd].at[h, :, rows, land], self.r_2.at[i, h])
 
-                @pl.loop(0, NZ)
+                @pl.loop(0, NZ, unroll=NZ)
                 def _(j):
                     a = self.view(ch, q, j, c, h)
                     a[...] = a[...] + self.r2[kd][h, j, rows, land]
@@ -642,8 +642,10 @@
     for d in greet:
         pl.semaphore_signal(barrier, inc=1, device_id=d, device_id_type=MESH)
     pl.semaphore_wait(barrier, len(greet))
-    for cp in loc:
+    for cp in loc[:4]:
         cp.wait()
+    for p in range(AHEAD):
+        G.begin(p)
 
     small, mix = r["small"], r["mix"]
     mix[...] = jnp.zeros_like(mix)
@@ -653,9 +655,9 @@
     small[t.s] = mix[...].astype(BF)
     for k in range(1, TEAM_S):
         S.go(small.at[t.s], small.at[t.s], r["ss"].at[0, k], r["sr"].at[0, k], others[k - 1])
-    for p in range(AHEAD):
-        G.begin(p)
     L.layout()
+    for cp in loc[4:]:
+        cp.wait()
     G.run(1, 0, 0)
     for k in range(1, TEAM_S):
         S.got(small.at[(t.s + TEAM_S - k) % TEAM_S], r["sr"].at[0, k])

time: 215 us -> 212 us (0.986)
  Pallas kernels: 211 us -> 208 us
    pallas_call x1, Pallas kernels: 205 us -> 203 us  [layer(): pl.pallas_call(functools.partial(layer_kernel, list(scratch), shards, tre...]
where the time goes in v2:
time: 212 us; the launch traced here: 209 us
  Pallas kernels  208 us (98%)
    pallas_call x1, Pallas kernels, layer(): pl.pallas_call(functools.partial(layer_kernel, list(scratch), shards, tre...  203 us
    pallas_call x1, Pallas kernels, finish(): pl.pallas_call(finish_kernel, out_shape=[sd(o.shape, BF) for o in outs[:3...  5.49 us

profile of v2, /device:TPU:0, one launch (start us, length us, event | category | flops | bytes accessed | tf_op | source)
XLA Modules:
  0.0 209.2 jit_solution(17584592946531252509)
XLA Ops:
  0.7 202.8 %decoder_layer.1 = (bf16[512,768]{1,0:T(8,128)(2,1)}, bf16[512,768]{1,0:T(8,128)(2,1)}, bf16[512,768]{1,0:T(8,128)(2,1)}, bf16[4,96,768]{2,1,0:T(8,128)(2,1)}, b...) custom-call(s32[2,13]{1,0:T(2,128)} %bitcast.24, ...), custom_call_target="tpu_custom_call" | custom-call | tf_op jit(solution)/shard_map/decoder_layer/pallas_call | solution.py:803
  203.4 5.5 %finish.1 = (bf16[512,768]{1,0:T(8,128)(2,1)}, bf16[512,768]{1,0:T(8,128)(2,1)}, bf16[512,768]{1,0:T(8,128)(2,1)}, f32[96,768]{1,0:T(8,128)}, f32[96,768]{1,0:T(...) custom-call(bf16[512,768]{1,0:T(8,128)(2,1)} %get-tuple-element.44.l, ...), custom_call_target="tpu_custom_call" | custom-call | tf_op jit(solution)/shard_map/finish/pallas_call | solution.py:856
